TPU v7x, 32 devices: a whole 2x2x4 slice. The times are simulated.
32 devices in a mesh: seg: 16 (over z, y, x), samp: 2 (over core).
Axes of the slice: x: 2, y: 2, z: 4, core: 2. Of those that a mesh axis runs over, the one named last changes fastest.
Arguments:
- rigidity_diagonal_cells: bfloat16 [512, 128, 128], P('seg')
- rigidity_lower_cells: bfloat16 [512, 128, 128], P('seg'), may hold values from -0.5 to 0.5
- inverse_diagonal_cells: bfloat16 [512, 128, 128], P('seg')
- bedding_rigidity_per_unknown: float32 [512, 128], P('seg'), may hold values from 0.3 to 2
- bedding_regime: int32 [512], P('seg'), may hold values from 0 to 2
- dilation_push_per_kelvin: float32 [512, 128], P('seg'), may hold values from 1 to 16
- heat_shape_functions: bfloat16 [512, 512], P('seg'), may hold values from -0.25 to 0.25
- sampled_shape_weights: bfloat16 [64, 512], P('samp'), may hold values from -6 to 6
- joined_segment_table: int32 [16, 2], P('seg'), may hold values from 0 to 15
- joint_rigidity: float32 [16, 2], P('seg'), may hold values from 1.2 to 3.6
Outputs:
- displacement: float32 [64, 512, 128], P('samp', 'seg')
- kl_grad: float32 [512], replicated
Inputs may be any that keep to these rules, and one draw needn't show every extreme that they name: `joined_segment_table`: every entry names a segment.
All inputs are finite; a program needn't handle non-finite values.
Results may differ from a plain program's by a relative error of at most 0.013.
Values may be sent and summed in bfloat16 or wider, within the bound.
A program may use at most 64 MiB of HBM per device.

v0:
```python
import math
import jax
import jax.numpy as jnp
from jax import lax
from jax.sharding import PartitionSpec as P

STEPS = 4


def shifted(value, axis, steps):
    count = lax.axis_size(axis)
    first, last = (max(0, -steps), min(count, count - steps))
    return lax.ppermute(value, axis, [(source, source + steps) for source in range(first, last)])


def stiffness(
    field_round, rigidity_diagonal_cells, rigidity_lower_cells, joined_segment_table, joint_rigidity
):
    own_term = jnp.einsum(
        "sjb,jab->sja", field_round, rigidity_diagonal_cells, preferred_element_type=jnp.float32
    )
    upward = jnp.einsum(
        "sjb,jba->sja", field_round, rigidity_lower_cells, preferred_element_type=jnp.float32
    ).astype(jnp.bfloat16)
    below_rim = shifted(field_round[:, -1:, :], "seg", 1)
    above_rim = shifted(upward[:, :1, :], "seg", -1)
    interfaces = lax.all_gather(field_round[:, :1, :], "seg", axis=1, tiled=True)
    lower_field = jnp.concatenate([below_rim, field_round[:, :-1]], axis=1)
    below_term = jnp.einsum(
        "sjb,jab->sja", lower_field, rigidity_lower_cells, preferred_element_type=jnp.float32
    )
    upper_term = jnp.concatenate([upward[:, 1:], above_rim], axis=1).astype(jnp.float32)
    result = own_term + below_term + upper_term
    partner = jnp.take(interfaces, joined_segment_table[0], axis=1).astype(jnp.float32)
    own_interface = field_round[:, 0:1, :].astype(jnp.float32)
    spring = jnp.sum(joint_rigidity[0][None, :, None] * (own_interface - partner), axis=1)
    return result.at[:, 0, :].add(spring)


def ballast(state, bedding_rigidity_per_unknown, bedding_regime):
    code = bedding_regime[None, :, None]
    stiff = bedding_rigidity_per_unknown[None]
    magnitude = 1.0 + jnp.abs(state)
    slide = jnp.tanh(state)
    force = jnp.where(
        code == 0, stiff * state, jnp.where(code == 1, stiff * state / magnitude, stiff * slide)
    )
    tangent = jnp.where(
        code == 0,
        stiff + 0.0 * state,
        jnp.where(code == 1, stiff / (magnitude * magnitude), stiff * (1.0 - slide * slide)),
    )
    return (force, tangent)


def blockwise(inverse_diagonal_cells, field_round):
    return jnp.einsum(
        "jab,sjb->sja", inverse_diagonal_cells, field_round, preferred_element_type=jnp.float32
    )


def body(
    rigidity_diagonal_cells,
    rigidity_lower_cells,
    inverse_diagonal_cells,
    bedding_rigidity_per_unknown,
    bedding_regime,
    dilation_push_per_kelvin,
    heat_shape_functions,
    sampled_shape_weights,
    joined_segment_table,
    joint_rigidity,
):
    samples_here = sampled_shape_weights.shape[0]
    blocks_here = rigidity_diagonal_cells.shape[0]
    width = rigidity_diagonal_cells.shape[1]
    shape_functions = heat_shape_functions.shape[1]
    complete_shape_functions = heat_shape_functions.astype(jnp.float32)
    heat_distribution = jnp.dot(
        sampled_shape_weights, heat_shape_functions.T, preferred_element_type=jnp.float32
    )
    heat_driven_source = dilation_push_per_kelvin[None] * heat_distribution[:, :, None]
    state = jnp.zeros((samples_here, blocks_here, width), jnp.float32)
    grad_total = jnp.zeros((shape_functions,), jnp.float32)
    for iteration in range(STEPS):
        state_round = state.astype(jnp.bfloat16)
        force, tangent = ballast(state, bedding_rigidity_per_unknown, bedding_regime)
        residual_vector = (
            heat_driven_source
            - stiffness(
                state_round,
                rigidity_diagonal_cells,
                rigidity_lower_cells,
                joined_segment_table,
                joint_rigidity,
            )
            - force
        )
        initial_newton_step = blockwise(
            inverse_diagonal_cells, residual_vector.astype(jnp.bfloat16)
        )
        second = (
            residual_vector
            - stiffness(
                initial_newton_step.astype(jnp.bfloat16),
                rigidity_diagonal_cells,
                rigidity_lower_cells,
                joined_segment_table,
                joint_rigidity,
            )
            - tangent * initial_newton_step
        )
        state = (
            state
            + initial_newton_step
            + blockwise(inverse_diagonal_cells, second.astype(jnp.bfloat16))
        )
        adjoint = jnp.einsum(
            "sja,jab->sjb",
            state.astype(jnp.bfloat16),
            inverse_diagonal_cells,
            preferred_element_type=jnp.float32,
        )
        weighted = jnp.sum(jnp.sum(dilation_push_per_kelvin[None] * adjoint, axis=2), axis=0)
        partial_value = jnp.dot(weighted, complete_shape_functions, precision=lax.Precision.HIGHEST)
        grad_total = grad_total + lax.psum(partial_value, ("seg", "samp"))
    every_block_list = blocks_here * lax.axis_size("seg")
    all_samples = samples_here * lax.axis_size("samp")
    scale = math.sqrt(shape_functions / (every_block_list * all_samples * width))
    return (state, grad_total * scale)


def solution(mesh):
    placed = (
        P("seg", None, None),
        P("seg", None, None),
        P("seg", None, None),
        P("seg", None),
        P("seg"),
        P("seg", None),
        P("seg", None),
        P("samp", None),
        P("seg", None),
        P("seg", None),
    )
    return jax.shard_map(
        body, mesh=mesh, in_specs=placed, out_specs=(P("samp", "seg", None), P()), check_vma=False
    )
```

profile of v0, /device:TPU:14, one launch (start us, length us, event | category | flops | bytes accessed | tf_op | source)
XLA Modules:
  0.0 460.8 jit_solution(1154479130879753834)
XLA Ops:
  0.7 3.5 collective-permute-start
  4.6 2.6 collective-permute-start.1
  17.6 4.8 %collective-permute-start.2 = (bf16[32,1,128]{2,0,1:T(8,128)(2,1)}, bf16[32,1,128]{2,0,1:T(8,128)(2,1)}, u32[]{:S(2)}, u32[]{:S(2)}) collective-permute-start(bf16[32,1,128]{2,0,1:T(8,128)(2,1)} %get-tuple-element.125), channel_id=1, source_target_pairs={{0,2},{2,4},{4,6},{6,8},{8,10},{10,12},{12,14},{14,16},{16,18},{18... | collective-permute-start | bytes 24584 | tf_op jit(solution)/shard_map/ppermute | solution.py:13
  22.4 30.9 %all_gather.22 = bf16[32,16,128]{2,0,1:T(8,128)(2,1)} all-gather(bf16[32,1,128]{2,0,1:T(8,128)(2,1)S(1)} %get-tuple-element.124), channel_id=1, replica_groups=mesh['seg'=16,'samp'=2] {'seg'}, dimensions={1}, use_global_device_ids=true | all-gather | bytes 139264 | tf_op jit(solution)/shard_map/all_gather | solution.py:27
  55.5 3.5 collective-permute-start.3
  59.1 4.1 collective-permute-done.3
  69.9 3.9 collective-permute-start.4
  73.8 34.6 %all_gather.23 = bf16[32,16,128]{2,0,1:T(8,128)(2,1)} all-gather(bf16[32,1,128]{2,0,1:T(8,128)(2,1)S(1)} %get-tuple-element.121), channel_id=1, replica_groups=mesh['seg'=16,'samp'=2] {'seg'}, dimensions={1}, use_global_device_ids=true | all-gather | bytes 139264 | tf_op jit(solution)/shard_map/all_gather | solution.py:27
  110.5 1.9 collective-permute-start.5
  112.6 5.3 %collective-permute-done.5 = bf16[32,1,128]{2,0,1:T(8,128)(2,1)S(1)} collective-permute-done((bf16[32,1,128]{2,0,1:T(8,128)(2,1)S(1)}, bf16[32,1,128]{2,0,1:T(8,128)(2,1)S(1)}, u32[]{:S(2)}, u32[]{:S(2)}) %collective-permute-start.5) | collective-permute-done | bytes 8224 | tf_op jit(solution)/shard_map/ppermute | solution.py:13
  124.6 1.9 collective-permute-start.6
  126.5 40.1 %all_gather.24 = bf16[32,16,128]{2,0,1:T(8,128)(2,1)} all-gather(bf16[32,1,128]{2,0,1:T(8,128)(2,1)S(1)} %get-tuple-element.118), channel_id=1, replica_groups=mesh['seg'=16,'samp'=2] {'seg'}, dimensions={1}, use_global_device_ids=true | all-gather | bytes 139264 | tf_op jit(solution)/shard_map/all_gather | solution.py:27
  168.8 1.9 collective-permute-start.7
  170.9 5.2 %collective-permute-done.7 = bf16[32,1,128]{2,0,1:T(8,128)(2,1)S(1)} collective-permute-done((bf16[32,1,128]{2,0,1:T(8,128)(2,1)S(1)}, bf16[32,1,128]{2,0,1:T(8,128)(2,1)S(1)}, u32[]{:S(2)}, u32[]{:S(2)}) %collective-permute-start.7) | collective-permute-done | bytes 8224 | tf_op jit(solution)/shard_map/ppermute | solution.py:13
  178.2 1.6 fusion.135
  184.1 1.9 collective-permute-start.8
  186.0 40.2 %all_gather.25 = bf16[32,16,128]{2,0,1:T(8,128)(2,1)} all-gather(bf16[32,1,128]{2,0,1:T(8,128)(2,1)S(1)} %get-tuple-element.115), channel_id=1, replica_groups=mesh['seg'=16,'samp'=2] {'seg'}, dimensions={1}, use_global_device_ids=true | all-gather | bytes 139264 | tf_op jit(solution)/shard_map/all_gather | solution.py:27
  228.4 1.9 collective-permute-start.9
  230.5 5.3 %collective-permute-done.9 = bf16[32,1,128]{2,0,1:T(8,128)(2,1)S(1)} collective-permute-done((bf16[32,1,128]{2,0,1:T(8,128)(2,1)S(1)}, bf16[32,1,128]{2,0,1:T(8,128)(2,1)S(1)}, u32[]{:S(2)}, u32[]{:S(2)}) %collective-permute-start.9) | collective-permute-done | bytes 8224 | tf_op jit(solution)/shard_map/ppermute | solution.py:13
  242.5 1.9 collective-permute-start.10
  244.4 40.1 %all_gather.26 = bf16[32,16,128]{2,0,1:T(8,128)(2,1)} all-gather(bf16[32,1,128]{2,0,1:T(8,128)(2,1)S(1)} %get-tuple-element.112), channel_id=1, replica_groups=mesh['seg'=16,'samp'=2] {'seg'}, dimensions={1}, use_global_device_ids=true | all-gather | bytes 139264 | tf_op jit(solution)/shard_map/all_gather | solution.py:27
  286.6 2.1 collective-permute-start.11
  288.9 5.0 %collective-permute-done.11 = bf16[32,1,128]{2,0,1:T(8,128)(2,1)S(1)} collective-permute-done((bf16[32,1,128]{2,0,1:T(8,128)(2,1)S(1)}, bf16[32,1,128]{2,0,1:T(8,128)(2,1)S(1)}, u32[]{:S(2)}, u32[]{:S(2)}) %collective-permute-start.11) | collective-permute-done | bytes 8224 | tf_op jit(solution)/shard_map/ppermute | solution.py:13
  301.9 1.9 collective-permute-start.12
  303.9 40.1 %all_gather.27 = bf16[32,16,128]{2,0,1:T(8,128)(2,1)} all-gather(bf16[32,1,128]{2,0,1:T(8,128)(2,1)S(1)} %get-tuple-element.109), channel_id=1, replica_groups=mesh['seg'=16,'samp'=2] {'seg'}, dimensions={1}, use_global_device_ids=true | all-gather | bytes 139264 | tf_op jit(solution)/shard_map/all_gather | solution.py:27
  346.1 2.0 collective-permute-start.13
  348.2 5.2 %collective-permute-done.13 = bf16[32,1,128]{2,0,1:T(8,128)(2,1)S(1)} collective-permute-done((bf16[32,1,128]{2,0,1:T(8,128)(2,1)S(1)}, bf16[32,1,128]{2,0,1:T(8,128)(2,1)S(1)}, u32[]{:S(2)}, u32[]{:S(2)}) %collective-permute-start.13) | collective-permute-done | bytes 8224 | tf_op jit(solution)/shard_map/ppermute | solution.py:13
  359.6 1.9 collective-permute-start.14
  361.5 37.3 %all_gather.28 = bf16[32,16,128]{2,0,1:T(8,128)(2,1)S(1)} all-gather(bf16[32,1,128]{2,0,1:T(8,128)(2,1)S(1)} %get-tuple-element.106), channel_id=1, replica_groups=mesh['seg'=16,'samp'=2] {'seg'}, dimensions={1}, use_global_device_ids=true | all-gather | bytes 139264 | tf_op jit(solution)/shard_map/all_gather | solution.py:27
  400.1 2.0 collective-permute-start.15
  402.2 5.2 %collective-permute-done.15 = bf16[32,1,128]{2,0,1:T(8,128)(2,1)S(1)} collective-permute-done((bf16[32,1,128]{2,0,1:T(8,128)(2,1)S(1)}, bf16[32,1,128]{2,0,1:T(8,128)(2,1)S(1)}, u32[]{:S(2)}, u32[]{:S(2)}) %collective-permute-start.15) | collective-permute-done | bytes 8224 | tf_op jit(solution)/shard_map/ppermute | solution.py:13
  412.1 48.0 %psum.34 = f32[512]{0:T(512)S(1)} all-reduce(f32[512]{0:T(512)S(1)} %add_add_fusion), channel_id=1, replica_groups=mesh['seg'=16,'samp'=2] {'seg','samp'}, use_global_device_ids=true, to_apply=%region_9.11 | all-reduce | flops 512 | bytes 4096 | tf_op jit(solution)/shard_map/psum | solution.py:126
  (226 shorter events, 71.2 us)
Async XLA Ops:
  0.6 7.8 %copy-start.1 = (bf16[32,128,128]{2,1,0:T(8,128)(2,1)S(1)}, bf16[32,128,128]{2,1,0:T(8,128)(2,1)}, u32[]{:S(2)}) copy-start(bf16[32,128,128]{2,1,0:T(8,128)(2,1)} %param.28) | copy-start | bytes 3145732
  0.7 10.2 %collective-permute-start = (bf16[32,1,128]{2,0,1:T(8,128)(2,1)S(1)}, bf16[32,1,128]{2,0,1:T(8,128)(2,1)S(1)}, u32[]{:S(2)}, u32[]{:S(2)}) collective-permute-start(bf16[32,1,128]{2,0,1:T(8,128)(2,1)S(1)} %slice.302), channel_id=1, source_target_pairs={{0,2},{2,4},{4,6},{6,8},{8,10},{10,12},{12,14},{14,16},{16,18},{18... | collective-permute-start | bytes 24584 | tf_op jit(solution)/shard_map/ppermute | solution.py:13
  4.6 7.5 %collective-permute-start.1 = (bf16[32,1,128]{2,0,1:T(8,128)(2,1)S(1)}, bf16[32,1,128]{2,0,1:T(8,128)(2,1)S(1)}, u32[]{:S(2)}, u32[]{:S(2)}) collective-permute-start(bf16[32,1,128]{2,0,1:T(8,128)(2,1)S(1)} %slice.366), channel_id=1, source_target_pairs={{2,0},{4,2},{6,4},{8,6},{10,8},{12,10},{14,12},{16,14},{18,16},{20... | collective-permute-start | bytes 24584 | tf_op jit(solution)/shard_map/ppermute | solution.py:13
  14.3 44.7 %copy-start.7 = (bf16[32,32,128]{2,0,1:T(8,128)(2,1)}, bf16[32,32,128]{2,0,1:T(8,128)(2,1)S(1)}, u32[]{:S(2)}) copy-start(bf16[32,32,128]{2,0,1:T(8,128)(2,1)S(1)} %convert_bitcast_fusion) | copy-start | bytes 786436
  17.6 41.5 %collective-permute-start.2 = (bf16[32,1,128]{2,0,1:T(8,128)(2,1)}, bf16[32,1,128]{2,0,1:T(8,128)(2,1)}, u32[]{:S(2)}, u32[]{:S(2)}) collective-permute-start(bf16[32,1,128]{2,0,1:T(8,128)(2,1)} %get-tuple-element.125), channel_id=1, source_target_pairs={{0,2},{2,4},{4,6},{6,8},{8,10},{10,12},{12,14},{14,16},{16,18},{18... | collective-permute-start | bytes 24584 | tf_op jit(solution)/shard_map/ppermute | solution.py:13
  55.5 7.7 %collective-permute-start.3 = (bf16[32,1,128]{2,0,1:T(8,128)(2,1)S(1)}, bf16[32,1,128]{2,0,1:T(8,128)(2,1)S(1)}, u32[]{:S(2)}, u32[]{:S(2)}) collective-permute-start(bf16[32,1,128]{2,0,1:T(8,128)(2,1)S(1)} %slice.371), channel_id=1, source_target_pairs={{2,0},{4,2},{6,4},{8,6},{10,8},{12,10},{14,12},{16,14},{18,16},{20... | collective-permute-start | bytes 24584 | tf_op jit(solution)/shard_map/ppermute | solution.py:13
  59.1 5.5 %copy-start.4 = (f32[32,32,128]{2,0,1:T(8,128)S(1)}, f32[32,32,128]{2,0,1:T(8,128)}, u32[]{:S(2)}) copy-start(f32[32,32,128]{2,0,1:T(8,128)} %copy-done.3) | copy-start | bytes 1572868
  59.1 5.5 %copy-start.6 = (f32[32,32,128]{2,1,0:T(8,128)S(1)}, f32[32,32,128]{2,1,0:T(8,128)}, u32[]{:S(2)}) copy-start(f32[32,32,128]{2,1,0:T(8,128)} %copy-done.5) | copy-start | bytes 1572868
  69.9 42.7 %collective-permute-start.4 = (bf16[32,1,128]{2,0,1:T(8,128)(2,1)}, bf16[32,1,128]{2,0,1:T(8,128)(2,1)}, u32[]{:S(2)}, u32[]{:S(2)}) collective-permute-start(bf16[32,1,128]{2,0,1:T(8,128)(2,1)} %get-tuple-element.122), channel_id=1, source_target_pairs={{0,2},{2,4},{4,6},{6,8},{8,10},{10,12},{12,14},{14,16},{16,18},{18... | collective-permute-start | bytes 24584 | tf_op jit(solution)/shard_map/ppermute | solution.py:13
  110.5 7.3 %collective-permute-start.5 = (bf16[32,1,128]{2,0,1:T(8,128)(2,1)S(1)}, bf16[32,1,128]{2,0,1:T(8,128)(2,1)S(1)}, u32[]{:S(2)}, u32[]{:S(2)}) collective-permute-start(bf16[32,1,128]{2,0,1:T(8,128)(2,1)S(1)} %slice.377), channel_id=1, source_target_pairs={{2,0},{4,2},{6,4},{8,6},{10,8},{12,10},{14,12},{16,14},{18,16},{20... | collective-permute-start | bytes 24584 | tf_op jit(solution)/shard_map/ppermute | solution.py:13
  112.6 6.7 %copy-start.24 = (f32[32,32,128]{2,0,1:T(8,128)S(1)}, f32[32,32,128]{2,0,1:T(8,128)}, u32[]{:S(2)}) copy-start(f32[32,32,128]{2,0,1:T(8,128)} %get-tuple-element.129) | copy-start | bytes 1572868
  124.6 46.3 %collective-permute-start.6 = (bf16[32,1,128]{2,0,1:T(8,128)(2,1)}, bf16[32,1,128]{2,0,1:T(8,128)(2,1)}, u32[]{:S(2)}, u32[]{:S(2)}) collective-permute-start(bf16[32,1,128]{2,0,1:T(8,128)(2,1)} %get-tuple-element.119), channel_id=1, source_target_pairs={{0,2},{2,4},{4,6},{6,8},{8,10},{10,12},{12,14},{14,16},{16,18},{18... | collective-permute-start | bytes 24584 | tf_op jit(solution)/shard_map/ppermute | solution.py:13
  168.8 7.3 %collective-permute-start.7 = (bf16[32,1,128]{2,0,1:T(8,128)(2,1)S(1)}, bf16[32,1,128]{2,0,1:T(8,128)(2,1)S(1)}, u32[]{:S(2)}, u32[]{:S(2)}) collective-permute-start(bf16[32,1,128]{2,0,1:T(8,128)(2,1)S(1)} %slice.383), channel_id=1, source_target_pairs={{2,0},{4,2},{6,4},{8,6},{10,8},{12,10},{14,12},{16,14},{18,16},{20... | collective-permute-start | bytes 24584 | tf_op jit(solution)/shard_map/ppermute | solution.py:13
  170.8 6.7 %copy-start.19 = (f32[32,32,128]{2,0,1:T(8,128)S(1)}, f32[32,32,128]{2,0,1:T(8,128)}, u32[]{:S(2)}) copy-start(f32[32,32,128]{2,0,1:T(8,128)} %copy-done.18) | copy-start | bytes 1572868
  170.9 6.7 %copy-start.25 = (f32[32,32,128]{2,0,1:T(8,128)S(1)}, f32[32,32,128]{2,0,1:T(8,128)}, u32[]{:S(2)}) copy-start(f32[32,32,128]{2,0,1:T(8,128)} %get-tuple-element.129) | copy-start | bytes 1572868
  170.9 6.7 %copy-start.50 = (f32[32,32,128]{2,0,1:T(8,128)S(1)}, f32[32,32,128]{2,0,1:T(8,128)}, u32[]{:S(2)}) copy-start(f32[32,32,128]{2,0,1:T(8,128)} %get-tuple-element.131) | copy-start | bytes 1572868
  184.1 46.4 %collective-permute-start.8 = (bf16[32,1,128]{2,0,1:T(8,128)(2,1)}, bf16[32,1,128]{2,0,1:T(8,128)(2,1)}, u32[]{:S(2)}, u32[]{:S(2)}) collective-permute-start(bf16[32,1,128]{2,0,1:T(8,128)(2,1)} %get-tuple-element.116), channel_id=1, source_target_pairs={{0,2},{2,4},{4,6},{6,8},{8,10},{10,12},{12,14},{14,16},{16,18},{18... | collective-permute-start | bytes 24584 | tf_op jit(solution)/shard_map/ppermute | solution.py:13
  228.4 7.3 %collective-permute-start.9 = (bf16[32,1,128]{2,0,1:T(8,128)(2,1)S(1)}, bf16[32,1,128]{2,0,1:T(8,128)(2,1)S(1)}, u32[]{:S(2)}, u32[]{:S(2)}) collective-permute-start(bf16[32,1,128]{2,0,1:T(8,128)(2,1)S(1)} %slice.389), channel_id=1, source_target_pairs={{2,0},{4,2},{6,4},{8,6},{10,8},{12,10},{14,12},{16,14},{18,16},{20... | collective-permute-start | bytes 24584 | tf_op jit(solution)/shard_map/ppermute | solution.py:13
  230.5 6.7 %copy-start.47 = (f32[32,32,128]{2,0,1:T(8,128)S(1)}, f32[32,32,128]{2,0,1:T(8,128)}, u32[]{:S(2)}) copy-start(f32[32,32,128]{2,0,1:T(8,128)} %get-tuple-element.133) | copy-start | bytes 1572868
  242.5 46.4 %collective-permute-start.10 = (bf16[32,1,128]{2,0,1:T(8,128)(2,1)}, bf16[32,1,128]{2,0,1:T(8,128)(2,1)}, u32[]{:S(2)}, u32[]{:S(2)}) collective-permute-start(bf16[32,1,128]{2,0,1:T(8,128)(2,1)} %get-tuple-element.113), channel_id=1, source_target_pairs={{0,2},{2,4},{4,6},{6,8},{8,10},{10,12},{12,14},{14,16},{16,18},{18... | collective-permute-start | bytes 24584 | tf_op jit(solution)/shard_map/ppermute | solution.py:13
  286.6 7.3 %collective-permute-start.11 = (bf16[32,1,128]{2,0,1:T(8,128)(2,1)S(1)}, bf16[32,1,128]{2,0,1:T(8,128)(2,1)S(1)}, u32[]{:S(2)}, u32[]{:S(2)}) collective-permute-start(bf16[32,1,128]{2,0,1:T(8,128)(2,1)S(1)} %slice.395), channel_id=1, source_target_pairs={{2,0},{4,2},{6,4},{8,6},{10,8},{12,10},{14,12},{16,14},{18,16},{20... | collective-permute-start | bytes 24584 | tf_op jit(solution)/shard_map/ppermute | solution.py:13
  288.9 6.5 %copy-start.21 = (f32[32,32,128]{2,0,1:T(8,128)S(1)}, f32[32,32,128]{2,0,1:T(8,128)}, u32[]{:S(2)}) copy-start(f32[32,32,128]{2,0,1:T(8,128)} %copy-done.20) | copy-start | bytes 1572868
  288.9 6.5 %copy-start.48 = (f32[32,32,128]{2,0,1:T(8,128)S(1)}, f32[32,32,128]{2,0,1:T(8,128)}, u32[]{:S(2)}) copy-start(f32[32,32,128]{2,0,1:T(8,128)} %get-tuple-element.133) | copy-start | bytes 1572868
  288.9 6.5 %copy-start.51 = (f32[32,32,128]{2,0,1:T(8,128)S(1)}, f32[32,32,128]{2,0,1:T(8,128)}, u32[]{:S(2)}) copy-start(f32[32,32,128]{2,0,1:T(8,128)} %get-tuple-element.135) | copy-start | bytes 1572868
  301.9 46.3 %collective-permute-start.12 = (bf16[32,1,128]{2,0,1:T(8,128)(2,1)}, bf16[32,1,128]{2,0,1:T(8,128)(2,1)}, u32[]{:S(2)}, u32[]{:S(2)}) collective-permute-start(bf16[32,1,128]{2,0,1:T(8,128)(2,1)} %get-tuple-element.110), channel_id=1, source_target_pairs={{0,2},{2,4},{4,6},{6,8},{8,10},{10,12},{12,14},{14,16},{16,18},{18... | collective-permute-start | bytes 24584 | tf_op jit(solution)/shard_map/ppermute | solution.py:13
  346.1 7.3 %collective-permute-start.13 = (bf16[32,1,128]{2,0,1:T(8,128)(2,1)S(1)}, bf16[32,1,128]{2,0,1:T(8,128)(2,1)S(1)}, u32[]{:S(2)}, u32[]{:S(2)}) collective-permute-start(bf16[32,1,128]{2,0,1:T(8,128)(2,1)S(1)} %slice.401), channel_id=1, source_target_pairs={{2,0},{4,2},{6,4},{8,6},{10,8},{12,10},{14,12},{16,14},{18,16},{20... | collective-permute-start | bytes 24584 | tf_op jit(solution)/shard_map/ppermute | solution.py:13
  348.2 6.7 %copy-start.45 = (f32[32,32,128]{2,0,1:T(8,128)S(1)}, f32[32,32,128]{2,0,1:T(8,128)}, u32[]{:S(2)}) copy-start(f32[32,32,128]{2,0,1:T(8,128)} %get-tuple-element.137) | copy-start | bytes 1572868
  359.6 42.6 %collective-permute-start.14 = (bf16[32,1,128]{2,0,1:T(8,128)(2,1)S(1)}, bf16[32,1,128]{2,0,1:T(8,128)(2,1)S(1)}, u32[]{:S(2)}, u32[]{:S(2)}) collective-permute-start(bf16[32,1,128]{2,0,1:T(8,128)(2,1)S(1)} %get-tuple-element.107), channel_id=1, source_target_pairs={{0,2},{2,4},{4,6},{6,8},{8,10},{10,12},{12,14},{14,16},{16,18},{18... | collective-permute-start | bytes 24584 | tf_op jit(solution)/shard_map/ppermute | solution.py:13
  400.1 7.3 %collective-permute-start.15 = (bf16[32,1,128]{2,0,1:T(8,128)(2,1)S(1)}, bf16[32,1,128]{2,0,1:T(8,128)(2,1)S(1)}, u32[]{:S(2)}, u32[]{:S(2)}) collective-permute-start(bf16[32,1,128]{2,0,1:T(8,128)(2,1)S(1)} %slice.407), channel_id=1, source_target_pairs={{2,0},{4,2},{6,4},{8,6},{10,8},{12,10},{14,12},{16,14},{18,16},{20... | collective-permute-start | bytes 24584 | tf_op jit(solution)/shard_map/ppermute | solution.py:13
  402.2 5.9 %copy-start.23 = (f32[32,32,128]{2,0,1:T(8,128)S(1)}, f32[32,32,128]{2,0,1:T(8,128)}, u32[]{:S(2)}) copy-start(f32[32,32,128]{2,0,1:T(8,128)} %copy-done.22) | copy-start | bytes 1572868
  402.2 5.9 %copy-start.46 = (f32[32,32,128]{2,0,1:T(8,128)S(1)}, f32[32,32,128]{2,0,1:T(8,128)}, u32[]{:S(2)}) copy-start(f32[32,32,128]{2,0,1:T(8,128)} %get-tuple-element.137) | copy-start | bytes 1572868
  402.2 5.9 %copy-start.49 = (f32[32,32,128]{2,0,1:T(8,128)S(1)}, f32[32,32,128]{2,0,1:T(8,128)}, u32[]{:S(2)}) copy-start(f32[32,32,128]{2,0,1:T(8,128)} %get-tuple-element.139) | copy-start | bytes 1572868
  (44 other events, 113.2 us)
where the time goes:
time: 462 us; the launch traced here: 461 us
  blocking collectives  311 us (67%)
  matrix products  43.6 us (9%)
  starting transfers between devices  39.7 us (9%)
  waiting for transfers between devices  36.5 us (8%)
  local copies, waits for them, and re-layouts  22.3 us (5%)
  other arithmetic  5.63 us (1%)
    all_gather x7, blocking collectives, stiffness(): lax.all_gather(field_round[:, :1, :], 'seg', axis=1, tiled=True)  263 us
    psum x1, blocking collectives, body(): grad_total = grad_total + lax.psum(partial_value, ('seg', 'samp'))  48 us
    ppermute x16, starting transfers between devices, shifted(): lax.ppermute(value, axis, [(source, source + steps) for source in range(f...  39.7 us
    ppermute x16, waiting for transfers between devices, shifted(): lax.ppermute(value, axis, [(source, source + steps) for source in range(f...  36.5 us
    dot_general x8, matrix products, stiffness(): jnp.einsum('sjb,jab->sja', field_round, rigidity_diagonal_cells, preferre...  11.7 us
    dot_general x8, matrix products, blockwise(): jnp.einsum('jab,sjb->sja', inverse_diagonal_cells, field_round, preferred...  10.8 us
    gather x8, local copies, waits for them, and re-layouts, stiffness(): jnp.take(interfaces, joined_segment_table[0], axis=1).astype(jnp.float32)  9.89 us
    dot_general x8, matrix products, stiffness(): jnp.einsum('sjb,jab->sja', lower_field, rigidity_lower_cells, preferred_e...  9.37 us
  transfers between devices with their start and end apart: 16, of which 8 were waited for; matrix products, arithmetic and copies ran while one was open for 4% of the time, Pallas kernels for 0%

commit v1 on v0

--- a/solution.py
+++ b/solution.py
@@ -24,7 +24,16 @@
     ).astype(jnp.bfloat16)
     below_rim = shifted(field_round[:, -1:, :], "seg", 1)
     above_rim = shifted(upward[:, :1, :], "seg", -1)
-    interfaces = lax.all_gather(field_round[:, :1, :], "seg", axis=1, tiled=True)
+    x = field_round[:, :1, :]
+    ways, here = (lax.axis_size("seg"), lax.axis_index("seg"))
+    grown, reach = (x, 1)
+    while reach < ways:
+        theirs = lax.ppermute(grown, "seg", [(d, d ^ reach) for d in range(ways)])
+        mine_first = jnp.concatenate([grown, theirs], axis=1)
+        theirs_first = jnp.concatenate([theirs, grown], axis=1)
+        grown = jnp.where(here & reach == 0, mine_first, theirs_first)
+        reach = 2 * reach
+    interfaces = grown
     lower_field = jnp.concatenate([below_rim, field_round[:, :-1]], axis=1)
     below_term = jnp.einsum(
         "sjb,jab->sja", lower_field, rigidity_lower_cells, preferred_element_type=jnp.float32

time: 462 us -> 265 us (0.57)
  blocking collectives: 311 us -> 38.6 us
  waiting for transfers between devices: 36.5 us -> 79.9 us
  starting transfers between devices: 39.7 us -> 74.7 us
  local copies, waits for them, and re-layouts: 22.3 us -> 7.16 us
  other arithmetic: 5.63 us -> 12.2 us
    all_gather x7 -> x0, blocking collectives: 263 us -> none  [stiffness(): lax.all_gather(field_round[:, :1, :], 'seg', axis=1, tiled=True)]
    ppermute x0 -> x32, waiting for transfers between devices: none -> 48 us  [stiffness(): theirs = lax.ppermute(grown, 'seg', [(d, d ^ reach) for d in range(ways)])]
    ppermute x0 -> x32, starting transfers between devices: none -> 19.6 us  [stiffness(): theirs = lax.ppermute(grown, 'seg', [(d, d ^ reach) for d in range(ways)])]
    ppermute x16, starting transfers between devices: 39.7 us -> 55 us  [shifted(): lax.ppermute(value, axis, [(source, source + steps) for source in range(f...]
    dot_general x8, matrix products: 10.8 us -> 22.2 us  [blockwise(): jnp.einsum('jab,sjb->sja', inverse_diagonal_cells, field_round, preferred...]
    scatter-add x8, other arithmetic: 0.12 us -> 10.6 us  [stiffness(): return result.at[:, 0, :].add(spring)]
    psum x1, blocking collectives: 48 us -> 38.6 us  [body(): grad_total = grad_total + lax.psum(partial_value, ('seg', 'samp'))]
    dot_general x8, matrix products: 11.7 us -> 5.97 us  [stiffness(): jnp.einsum('sjb,jab->sja', field_round, rigidity_diagonal_cells, preferre...]
  transfers between devices with their start and end apart: 16 -> 48, of which waited for: 8 -> 24; matrix products, arithmetic and copies ran while one was open for 4% -> 9% of each run, Pallas kernels for 0% -> 0%
where the time goes in v1:
time: 265 us; the launch traced here: 260 us
  waiting for transfers between devices  79.9 us (30%)
  starting transfers between devices  74.7 us (28%)
  matrix products  46.5 us (18%)
  blocking collectives  38.6 us (15%)
  other arithmetic  12.2 us (5%)
  local copies, waits for them, and re-layouts  7.16 us (3%)
    ppermute x16, starting transfers between devices, shifted(): lax.ppermute(value, axis, [(source, source + steps) for source in range(f...  55 us
    ppermute x32, waiting for transfers between devices, stiffness(): theirs = lax.ppermute(grown, 'seg', [(d, d ^ reach) for d in range(ways)])  48 us
    psum x1, blocking collectives, body(): grad_total = grad_total + lax.psum(partial_value, ('seg', 'samp'))  38.6 us
    ppermute x16, waiting for transfers between devices, shifted(): lax.ppermute(value, axis, [(source, source + steps) for source in range(f...  31.9 us
    dot_general x8, matrix products, blockwise(): jnp.einsum('jab,sjb->sja', inverse_diagonal_cells, field_round, preferred...  22.2 us
    ppermute x32, starting transfers between devices, stiffness(): theirs = lax.ppermute(grown, 'seg', [(d, d ^ reach) for d in range(ways)])  19.6 us
    dot_general x8, matrix products, stiffness(): jnp.einsum('sjb,jab->sja', lower_field, rigidity_lower_cells, preferred_e...  12.7 us
    scatter-add x8, other arithmetic, stiffness(): return result.at[:, 0, :].add(spring)  10.6 us
  transfers between devices with their start and end apart: 48, of which 24 were waited for; matrix products, arithmetic and copies ran while one was open for 9% of the time, Pallas kernels for 0%

profile of v1, /device:TPU:14, one launch (start us, length us, event | category | flops | bytes accessed | tf_op | source)
XLA Modules:
  0.0 260.4 jit_solution(14433772564318698069)
XLA Ops:
  1.3 4.3 %collective-permute-start = (bf16[32,1,128]{2,0,1:T(8,128)(2,1)S(1)}, bf16[32,1,128]{2,0,1:T(8,128)(2,1)S(1)}, u32[]{:S(2)}, u32[]{:S(2)}) collective-permute-start(bf16[32,1,128]{2,0,1:T(8,128)(2,1)S(1)} %slice.300), channel_id=1, source_target_pairs={{0,2},{2,4},{4,6},{6,8},{8,10},{10,12},{12,14},{14,16},{16,18},{18... | collective-permute-start | bytes 24584 | tf_op jit(solution)/shard_map/ppermute | solution.py:13
  10.9 3.2 %collective-permute-done.3 = bf16[32,2,128]{2,0,1:T(8,128)(2,1)S(1)} collective-permute-done((bf16[32,2,128]{2,0,1:T(8,128)(2,1)S(1)}, bf16[32,2,128]{2,0,1:T(8,128)(2,1)S(1)}, u32[]{:S(2)}, u32[]{:S(2)}) %collective-permute-start.3) | collective-permute-done | bytes 16416 | tf_op jit(solution)/shard_map/ppermute | solution.py:31
  14.6 3.4 %collective-permute-done.4 = bf16[32,4,128]{2,0,1:T(8,128)(2,1)S(1)} collective-permute-done((bf16[32,4,128]{2,0,1:T(8,128)(2,1)S(1)}, bf16[32,4,128]{2,0,1:T(8,128)(2,1)S(1)}, u32[]{:S(2)}, u32[]{:S(2)}) %collective-permute-start.4) | collective-permute-done | bytes 32800 | tf_op jit(solution)/shard_map/ppermute | solution.py:31
  36.5 7.4 %collective-permute-start.6 = (bf16[32,1,128]{2,0,1:T(8,128)(2,1)S(1)}, bf16[32,1,128]{2,0,1:T(8,128)(2,1)S(1)}, u32[]{:S(2)}, u32[]{:S(2)}) collective-permute-start(bf16[32,1,128]{2,0,1:T(8,128)(2,1)S(1)} %get-tuple-element.123), channel_id=1, source_target_pairs={{0,2},{2,4},{4,6},{6,8},{8,10},{10,12},{12,14},{14,16},{16,18},{18... | collective-permute-start | bytes 24584 | tf_op jit(solution)/shard_map/ppermute | solution.py:13
  46.0 5.8 %collective-permute-done.7 = bf16[32,1,128]{2,0,1:T(8,128)(2,1)S(1)} collective-permute-done((bf16[32,1,128]{2,0,1:T(8,128)(2,1)S(1)}, bf16[32,1,128]{2,0,1:T(8,128)(2,1)S(1)}, u32[]{:S(2)}, u32[]{:S(2)}) %collective-permute-start.7) | collective-permute-done | bytes 8224 | tf_op jit(solution)/shard_map/ppermute | solution.py:13
  55.2 3.0 %fusion.133 = (bf16[32,32,128]{2,0,1:T(8,128)(2,1)S(1)}, f32[32,32,128]{2,0,1:T(8,128)}) fusion(f32[32,32,128]{2,1,0:T(8,128)} %copy-done.3, bf16[32,128,128]{2,1,0:T(8,128)(2,1)S(1)} %copy-done.2, f32[32,32,128]{2,0,1:T(8,128)} %fusion.102, f32[32,32,128]{2,0,1:T(8,128)} %fusion.103, f32[32,128]{1,0:T(8,128)S(1)} %copy-done.7, ...), kind=kOutput, calls=%fused_computation.234 | convolution fusion | flops 34734080 | bytes 3461120 | tf_op jit(solution)/shard_map/jab,sjb->sja/dot_general | solution.py:66
  58.9 3.0 %collective-permute-done.14 = bf16[32,1,128]{2,0,1:T(8,128)(2,1)S(1)} collective-permute-done((bf16[32,1,128]{2,0,1:T(8,128)(2,1)S(1)}, bf16[32,1,128]{2,0,1:T(8,128)(2,1)S(1)}, u32[]{:S(2)}, u32[]{:S(2)}) %collective-permute-start.14) | collective-permute-done | bytes 8224 | tf_op jit(solution)/shard_map/ppermute | solution.py:31
  62.3 3.4 %collective-permute-done.15 = bf16[32,2,128]{2,0,1:T(8,128)(2,1)S(1)} collective-permute-done((bf16[32,2,128]{2,0,1:T(8,128)(2,1)S(1)}, bf16[32,2,128]{2,0,1:T(8,128)(2,1)S(1)}, u32[]{:S(2)}, u32[]{:S(2)}) %collective-permute-start.15) | collective-permute-done | bytes 16416 | tf_op jit(solution)/shard_map/ppermute | solution.py:31
  66.3 3.7 %collective-permute-start.12 = (bf16[32,1,128]{2,0,1:T(8,128)(2,1)S(1)}, bf16[32,1,128]{2,0,1:T(8,128)(2,1)S(1)}, u32[]{:S(2)}, u32[]{:S(2)}) collective-permute-start(bf16[32,1,128]{2,0,1:T(8,128)(2,1)S(1)} %get-tuple-element.120), channel_id=1, source_target_pairs={{0,2},{2,4},{4,6},{6,8},{8,10},{10,12},{12,14},{14,16},{16,18},{18... | collective-permute-start | bytes 24584 | tf_op jit(solution)/shard_map/ppermute | solution.py:13
  73.3 4.0 %collective-permute-done.13 = bf16[32,1,128]{2,0,1:T(8,128)(2,1)S(1)} collective-permute-done((bf16[32,1,128]{2,0,1:T(8,128)(2,1)S(1)}, bf16[32,1,128]{2,0,1:T(8,128)(2,1)S(1)}, u32[]{:S(2)}, u32[]{:S(2)}) %collective-permute-start.13) | collective-permute-done | bytes 8224 | tf_op jit(solution)/shard_map/ppermute | solution.py:13
  83.6 3.5 %collective-permute-done.20 = bf16[32,1,128]{2,0,1:T(8,128)(2,1)S(1)} collective-permute-done((bf16[32,1,128]{2,0,1:T(8,128)(2,1)S(1)}, bf16[32,1,128]{2,0,1:T(8,128)(2,1)S(1)}, u32[]{:S(2)}, u32[]{:S(2)}) %collective-permute-start.20) | collective-permute-done | bytes 8224 | tf_op jit(solution)/shard_map/ppermute | solution.py:31
  88.0 2.9 %collective-permute-done.21 = bf16[32,2,128]{2,0,1:T(8,128)(2,1)S(1)} collective-permute-done((bf16[32,2,128]{2,0,1:T(8,128)(2,1)S(1)}, bf16[32,2,128]{2,0,1:T(8,128)(2,1)S(1)}, u32[]{:S(2)}, u32[]{:S(2)}) %collective-permute-start.21) | collective-permute-done | bytes 16416 | tf_op jit(solution)/shard_map/ppermute | solution.py:31
  92.3 5.3 %collective-permute-start.18 = (bf16[32,1,128]{2,0,1:T(8,128)(2,1)S(1)}, bf16[32,1,128]{2,0,1:T(8,128)(2,1)S(1)}, u32[]{:S(2)}, u32[]{:S(2)}) collective-permute-start(bf16[32,1,128]{2,0,1:T(8,128)(2,1)S(1)} %get-tuple-element.117), channel_id=1, source_target_pairs={{0,2},{2,4},{4,6},{6,8},{8,10},{10,12},{12,14},{14,16},{16,18},{18... | collective-permute-start | bytes 24584 | tf_op jit(solution)/shard_map/ppermute | solution.py:13
  100.7 4.4 %collective-permute-done.19 = bf16[32,1,128]{2,0,1:T(8,128)(2,1)S(1)} collective-permute-done((bf16[32,1,128]{2,0,1:T(8,128)(2,1)S(1)}, bf16[32,1,128]{2,0,1:T(8,128)(2,1)S(1)}, u32[]{:S(2)}, u32[]{:S(2)}) %collective-permute-start.19) | collective-permute-done | bytes 8224 | tf_op jit(solution)/shard_map/ppermute | solution.py:13
  108.5 3.5 %fusion.135 = (bf16[32,32,128]{2,0,1:T(8,128)(2,1)S(1)}, f32[32,32,128]{2,0,1:T(8,128)}) fusion(bf16[32,128,128]{2,1,0:T(8,128)(2,1)S(1)} %copy-done.2, f32[32,32,128]{2,0,1:T(8,128)} %get-tuple-element.129, f32[32,32,128]{2,0,1:T(8,128)} %get-tuple-element.127, f32[32,32,128]{2,0,1:T(8,128)} %fusion.100, f32[32,128]{1,0:T(8,128)S(1)} %copy-done.7, ...), kind=kOutput, calls=%fused_computation.236 | convolution fusion | flops 36962304 | bytes 3969088 | tf_op jit(solution)/shard_map/jab,sjb->sja/dot_general | solution.py:66
  112.7 3.0 %collective-permute-done.26 = bf16[32,1,128]{2,0,1:T(8,128)(2,1)S(1)} collective-permute-done((bf16[32,1,128]{2,0,1:T(8,128)(2,1)S(1)}, bf16[32,1,128]{2,0,1:T(8,128)(2,1)S(1)}, u32[]{:S(2)}, u32[]{:S(2)}) %collective-permute-start.26) | collective-permute-done | bytes 8224 | tf_op jit(solution)/shard_map/ppermute | solution.py:31
  116.0 3.4 %collective-permute-done.27 = bf16[32,2,128]{2,0,1:T(8,128)(2,1)S(1)} collective-permute-done((bf16[32,2,128]{2,0,1:T(8,128)(2,1)S(1)}, bf16[32,2,128]{2,0,1:T(8,128)(2,1)S(1)}, u32[]{:S(2)}, u32[]{:S(2)}) %collective-permute-start.27) | collective-permute-done | bytes 16416 | tf_op jit(solution)/shard_map/ppermute | solution.py:31
  120.1 4.0 %collective-permute-start.24 = (bf16[32,1,128]{2,0,1:T(8,128)(2,1)S(1)}, bf16[32,1,128]{2,0,1:T(8,128)(2,1)S(1)}, u32[]{:S(2)}, u32[]{:S(2)}) collective-permute-start(bf16[32,1,128]{2,0,1:T(8,128)(2,1)S(1)} %get-tuple-element.114), channel_id=1, source_target_pairs={{0,2},{2,4},{4,6},{6,8},{8,10},{10,12},{12,14},{14,16},{16,18},{18... | collective-permute-start | bytes 24584 | tf_op jit(solution)/shard_map/ppermute | solution.py:13
  127.6 3.9 %collective-permute-done.25 = bf16[32,1,128]{2,0,1:T(8,128)(2,1)S(1)} collective-permute-done((bf16[32,1,128]{2,0,1:T(8,128)(2,1)S(1)}, bf16[32,1,128]{2,0,1:T(8,128)(2,1)S(1)}, u32[]{:S(2)}, u32[]{:S(2)}) %collective-permute-start.25) | collective-permute-done | bytes 8224 | tf_op jit(solution)/shard_map/ppermute | solution.py:13
  137.7 3.5 %collective-permute-done.32 = bf16[32,1,128]{2,0,1:T(8,128)(2,1)S(1)} collective-permute-done((bf16[32,1,128]{2,0,1:T(8,128)(2,1)S(1)}, bf16[32,1,128]{2,0,1:T(8,128)(2,1)S(1)}, u32[]{:S(2)}, u32[]{:S(2)}) %collective-permute-start.32) | collective-permute-done | bytes 8224 | tf_op jit(solution)/shard_map/ppermute | solution.py:31
  146.6 5.3 %collective-permute-start.30 = (bf16[32,1,128]{2,0,1:T(8,128)(2,1)S(1)}, bf16[32,1,128]{2,0,1:T(8,128)(2,1)S(1)}, u32[]{:S(2)}, u32[]{:S(2)}) collective-permute-start(bf16[32,1,128]{2,0,1:T(8,128)(2,1)S(1)} %get-tuple-element.111), channel_id=1, source_target_pairs={{0,2},{2,4},{4,6},{6,8},{8,10},{10,12},{12,14},{14,16},{16,18},{18... | collective-permute-start | bytes 24584 | tf_op jit(solution)/shard_map/ppermute | solution.py:13
  155.0 5.1 %collective-permute-done.31 = bf16[32,1,128]{2,0,1:T(8,128)(2,1)S(1)} collective-permute-done((bf16[32,1,128]{2,0,1:T(8,128)(2,1)S(1)}, bf16[32,1,128]{2,0,1:T(8,128)(2,1)S(1)}, u32[]{:S(2)}, u32[]{:S(2)}) %collective-permute-start.31) | collective-permute-done | bytes 8224 | tf_op jit(solution)/shard_map/ppermute | solution.py:13
  163.5 3.4 %fusion.137 = (bf16[32,32,128]{2,0,1:T(8,128)(2,1)S(1)}, f32[32,32,128]{2,0,1:T(8,128)}) fusion(bf16[32,128,128]{2,1,0:T(8,128)(2,1)S(1)} %copy-done.2, f32[32,32,128]{2,0,1:T(8,128)} %get-tuple-element.133, f32[32,32,128]{2,0,1:T(8,128)} %get-tuple-element.131, f32[32,32,128]{2,0,1:T(8,128)} %fusion.98, f32[32,128]{1,0:T(8,128)S(1)} %copy-done.7, ...), kind=kOutput, calls=%fused_computation.238 | convolution fusion | flops 36962304 | bytes 3969088 | tf_op jit(solution)/shard_map/jab,sjb->sja/dot_general | solution.py:66
  167.6 3.0 %collective-permute-done.38 = bf16[32,1,128]{2,0,1:T(8,128)(2,1)S(1)} collective-permute-done((bf16[32,1,128]{2,0,1:T(8,128)(2,1)S(1)}, bf16[32,1,128]{2,0,1:T(8,128)(2,1)S(1)}, u32[]{:S(2)}, u32[]{:S(2)}) %collective-permute-start.38) | collective-permute-done | bytes 8224 | tf_op jit(solution)/shard_map/ppermute | solution.py:31
  170.9 3.4 %collective-permute-done.39 = bf16[32,2,128]{2,0,1:T(8,128)(2,1)S(1)} collective-permute-done((bf16[32,2,128]{2,0,1:T(8,128)(2,1)S(1)}, bf16[32,2,128]{2,0,1:T(8,128)(2,1)S(1)}, u32[]{:S(2)}, u32[]{:S(2)}) %collective-permute-start.39) | collective-permute-done | bytes 16416 | tf_op jit(solution)/shard_map/ppermute | solution.py:31
  175.0 3.6 %collective-permute-start.36 = (bf16[32,1,128]{2,0,1:T(8,128)(2,1)S(1)}, bf16[32,1,128]{2,0,1:T(8,128)(2,1)S(1)}, u32[]{:S(2)}, u32[]{:S(2)}) collective-permute-start(bf16[32,1,128]{2,0,1:T(8,128)(2,1)S(1)} %get-tuple-element.108), channel_id=1, source_target_pairs={{0,2},{2,4},{4,6},{6,8},{8,10},{10,12},{12,14},{14,16},{16,18},{18... | collective-permute-start | bytes 24584 | tf_op jit(solution)/shard_map/ppermute | solution.py:13
  181.6 4.2 %collective-permute-done.37 = bf16[32,1,128]{2,0,1:T(8,128)(2,1)S(1)} collective-permute-done((bf16[32,1,128]{2,0,1:T(8,128)(2,1)S(1)}, bf16[32,1,128]{2,0,1:T(8,128)(2,1)S(1)}, u32[]{:S(2)}, u32[]{:S(2)}) %collective-permute-start.37) | collective-permute-done | bytes 8224 | tf_op jit(solution)/shard_map/ppermute | solution.py:13
  189.3 2.7 %fusion.138 = (bf16[32,32,128]{2,0,1:T(8,128)(2,1)S(1)}, f32[32,32,128]{2,0,1:T(8,128)}) fusion(bf16[32,128,128]{2,1,0:T(8,128)(2,1)S(1)} %copy-done.2, f32[32,32,128]{2,0,1:T(8,128)} %get-tuple-element.135, pred[32]{0:T(512)(128)(4,1)S(1)} %get-tuple-element.125, f32[32,128]{1,0:T(8,128)S(1)} %copy-done.7, pred[32]{0:T(512)(128)(4,1)S(1)} %get-tuple-element.124, ...), kind=kOutput, calls=%fused_computation.239 | convolution fusion | flops 35127296 | bytes 2920512 | tf_op jit(solution)/shard_map/jab,sjb->sja/dot_general | solution.py:66
  192.2 3.4 %collective-permute-done.44 = bf16[32,1,128]{2,0,1:T(8,128)(2,1)S(1)} collective-permute-done((bf16[32,1,128]{2,0,1:T(8,128)(2,1)S(1)}, bf16[32,1,128]{2,0,1:T(8,128)(2,1)S(1)}, u32[]{:S(2)}, u32[]{:S(2)}) %collective-permute-start.44) | collective-permute-done | bytes 8224 | tf_op jit(solution)/shard_map/ppermute | solution.py:31
  201.2 5.0 %collective-permute-start.42 = (bf16[32,1,128]{2,0,1:T(8,128)(2,1)S(1)}, bf16[32,1,128]{2,0,1:T(8,128)(2,1)S(1)}, u32[]{:S(2)}, u32[]{:S(2)}) collective-permute-start(bf16[32,1,128]{2,0,1:T(8,128)(2,1)S(1)} %get-tuple-element.105), channel_id=1, source_target_pairs={{0,2},{2,4},{4,6},{6,8},{8,10},{10,12},{12,14},{14,16},{16,18},{18... | collective-permute-start | bytes 24584 | tf_op jit(solution)/shard_map/ppermute | solution.py:13
  209.1 4.4 %collective-permute-done.43 = bf16[32,1,128]{2,0,1:T(8,128)(2,1)S(1)} collective-permute-done((bf16[32,1,128]{2,0,1:T(8,128)(2,1)S(1)}, bf16[32,1,128]{2,0,1:T(8,128)(2,1)S(1)}, u32[]{:S(2)}, u32[]{:S(2)}) %collective-permute-start.43) | collective-permute-done | bytes 8224 | tf_op jit(solution)/shard_map/ppermute | solution.py:13
  221.3 38.6 %psum.34 = f32[512]{0:T(512)S(1)} all-reduce(f32[512]{0:T(512)S(1)} %add_add_fusion), channel_id=1, replica_groups=mesh['seg'=16,'samp'=2] {'seg','samp'}, use_global_device_ids=true, to_apply=%region_9.11 | all-reduce | flops 512 | bytes 4096 | tf_op jit(solution)/shard_map/psum | solution.py:135
  (227 shorter events, 98.3 us)
Async XLA Ops:
  0.7 9.6 %collective-permute-start.2 = (bf16[32,1,128]{2,0,1:T(8,128)(2,1)S(1)}, bf16[32,1,128]{2,0,1:T(8,128)(2,1)S(1)}, u32[]{:S(2)}, u32[]{:S(2)}) collective-permute-start(bf16[32,1,128]{2,0,1:T(8,128)(2,1)S(1)} %slice.300), channel_id=1, source_target_pairs={{0,2},{2,0},{4,6},{6,4},{8,10},{10,8},{12,14},{14,12},{16,18},{18,... | collective-permute-start | bytes 24584 | tf_op jit(solution)/shard_map/ppermute | solution.py:31
  1.3 19.0 %collective-permute-start = (bf16[32,1,128]{2,0,1:T(8,128)(2,1)S(1)}, bf16[32,1,128]{2,0,1:T(8,128)(2,1)S(1)}, u32[]{:S(2)}, u32[]{:S(2)}) collective-permute-start(bf16[32,1,128]{2,0,1:T(8,128)(2,1)S(1)} %slice.300), channel_id=1, source_target_pairs={{0,2},{2,4},{4,6},{6,8},{8,10},{10,12},{12,14},{14,16},{16,18},{18... | collective-permute-start | bytes 24584 | tf_op jit(solution)/shard_map/ppermute | solution.py:13
  6.0 14.3 %collective-permute-start.1 = (bf16[32,1,128]{2,0,1:T(8,128)(2,1)S(1)}, bf16[32,1,128]{2,0,1:T(8,128)(2,1)S(1)}, u32[]{:S(2)}, u32[]{:S(2)}) collective-permute-start(bf16[32,1,128]{2,0,1:T(8,128)(2,1)S(1)} %slice.363), channel_id=1, source_target_pairs={{2,0},{4,2},{6,4},{8,6},{10,8},{12,10},{14,12},{16,14},{18,16},{20... | collective-permute-start | bytes 24584 | tf_op jit(solution)/shard_map/ppermute | solution.py:13
  18.1 5.2 %collective-permute-start.5 = (bf16[32,8,128]{2,0,1:T(8,128)(2,1)S(1)}, bf16[32,8,128]{2,0,1:T(8,128)(2,1)S(1)}, u32[]{:S(2)}, u32[]{:S(2)}) collective-permute-start(bf16[32,8,128]{2,0,1:T(8,128)(2,1)S(1)} %maximum_select_fusion.8), channel_id=1, source_target_pairs={{0,16},{2,18},{4,20},{6,22},{8,24},{10,26},{12,28},{14,30},{16,0},... | collective-permute-start | bytes 196616 | tf_op jit(solution)/shard_map/ppermute | solution.py:31
  35.3 10.6 %collective-permute-start.10 = (bf16[32,4,128]{2,0,1:T(8,128)(2,1)S(1)}, bf16[32,4,128]{2,0,1:T(8,128)(2,1)S(1)}, u32[]{:S(2)}, u32[]{:S(2)}) collective-permute-start(bf16[32,4,128]{2,0,1:T(8,128)(2,1)S(1)} %maximum_select_fusion.17), channel_id=1, source_target_pairs={{0,8},{2,10},{4,12},{6,14},{8,0},{10,2},{12,4},{14,6},{16,24},{18,... | collective-permute-start | bytes 98312 | tf_op jit(solution)/shard_map/ppermute | solution.py:31
  36.5 9.5 %collective-permute-start.6 = (bf16[32,1,128]{2,0,1:T(8,128)(2,1)S(1)}, bf16[32,1,128]{2,0,1:T(8,128)(2,1)S(1)}, u32[]{:S(2)}, u32[]{:S(2)}) collective-permute-start(bf16[32,1,128]{2,0,1:T(8,128)(2,1)S(1)} %get-tuple-element.123), channel_id=1, source_target_pairs={{0,2},{2,4},{4,6},{6,8},{8,10},{10,12},{12,14},{14,16},{16,18},{18... | collective-permute-start | bytes 24584 | tf_op jit(solution)/shard_map/ppermute | solution.py:13
  43.9 7.9 %collective-permute-start.7 = (bf16[32,1,128]{2,0,1:T(8,128)(2,1)S(1)}, bf16[32,1,128]{2,0,1:T(8,128)(2,1)S(1)}, u32[]{:S(2)}, u32[]{:S(2)}) collective-permute-start(bf16[32,1,128]{2,0,1:T(8,128)(2,1)S(1)} %slice.368), channel_id=1, source_target_pairs={{2,0},{4,2},{6,4},{8,6},{10,8},{12,10},{14,12},{16,14},{18,16},{20... | collective-permute-start | bytes 24584 | tf_op jit(solution)/shard_map/ppermute | solution.py:13
  45.9 7.4 %collective-permute-start.11 = (bf16[32,8,128]{2,0,1:T(8,128)(2,1)S(1)}, bf16[32,8,128]{2,0,1:T(8,128)(2,1)S(1)}, u32[]{:S(2)}, u32[]{:S(2)}) collective-permute-start(bf16[32,8,128]{2,0,1:T(8,128)(2,1)S(1)} %maximum_select_fusion.9), channel_id=1, source_target_pairs={{0,16},{2,18},{4,20},{6,22},{8,24},{10,26},{12,28},{14,30},{16,0},... | collective-permute-start | bytes 196616 | tf_op jit(solution)/shard_map/ppermute | solution.py:31
  65.7 6.5 %collective-permute-start.16 = (bf16[32,4,128]{2,0,1:T(8,128)(2,1)S(1)}, bf16[32,4,128]{2,0,1:T(8,128)(2,1)S(1)}, u32[]{:S(2)}, u32[]{:S(2)}) collective-permute-start(bf16[32,4,128]{2,0,1:T(8,128)(2,1)S(1)} %maximum_select_fusion.18), channel_id=1, source_target_pairs={{0,8},{2,10},{4,12},{6,14},{8,0},{10,2},{12,4},{14,6},{16,24},{18,... | collective-permute-start | bytes 98312 | tf_op jit(solution)/shard_map/ppermute | solution.py:31
  66.3 7.0 %collective-permute-start.12 = (bf16[32,1,128]{2,0,1:T(8,128)(2,1)S(1)}, bf16[32,1,128]{2,0,1:T(8,128)(2,1)S(1)}, u32[]{:S(2)}, u32[]{:S(2)}) collective-permute-start(bf16[32,1,128]{2,0,1:T(8,128)(2,1)S(1)} %get-tuple-element.120), channel_id=1, source_target_pairs={{0,2},{2,4},{4,6},{6,8},{8,10},{10,12},{12,14},{14,16},{16,18},{18... | collective-permute-start | bytes 24584 | tf_op jit(solution)/shard_map/ppermute | solution.py:13
  70.0 7.3 %collective-permute-start.13 = (bf16[32,1,128]{2,0,1:T(8,128)(2,1)S(1)}, bf16[32,1,128]{2,0,1:T(8,128)(2,1)S(1)}, u32[]{:S(2)}, u32[]{:S(2)}) collective-permute-start(bf16[32,1,128]{2,0,1:T(8,128)(2,1)S(1)} %slice.374), channel_id=1, source_target_pairs={{2,0},{4,2},{6,4},{8,6},{10,8},{12,10},{14,12},{16,14},{18,16},{20... | collective-permute-start | bytes 24584 | tf_op jit(solution)/shard_map/ppermute | solution.py:13
  72.2 6.6 %collective-permute-start.17 = (bf16[32,8,128]{2,0,1:T(8,128)(2,1)S(1)}, bf16[32,8,128]{2,0,1:T(8,128)(2,1)S(1)}, u32[]{:S(2)}, u32[]{:S(2)}) collective-permute-start(bf16[32,8,128]{2,0,1:T(8,128)(2,1)S(1)} %maximum_select_fusion.10), channel_id=1, source_target_pairs={{0,16},{2,18},{4,20},{6,22},{8,24},{10,26},{12,28},{14,30},{16,0},... | collective-permute-start | bytes 196616 | tf_op jit(solution)/shard_map/ppermute | solution.py:31
  90.9 8.8 %collective-permute-start.22 = (bf16[32,4,128]{2,0,1:T(8,128)(2,1)S(1)}, bf16[32,4,128]{2,0,1:T(8,128)(2,1)S(1)}, u32[]{:S(2)}, u32[]{:S(2)}) collective-permute-start(bf16[32,4,128]{2,0,1:T(8,128)(2,1)S(1)} %maximum_select_fusion.19), channel_id=1, source_target_pairs={{0,8},{2,10},{4,12},{6,14},{8,0},{10,2},{12,4},{14,6},{16,24},{18,... | collective-permute-start | bytes 98312 | tf_op jit(solution)/shard_map/ppermute | solution.py:31
  92.3 8.4 %collective-permute-start.18 = (bf16[32,1,128]{2,0,1:T(8,128)(2,1)S(1)}, bf16[32,1,128]{2,0,1:T(8,128)(2,1)S(1)}, u32[]{:S(2)}, u32[]{:S(2)}) collective-permute-start(bf16[32,1,128]{2,0,1:T(8,128)(2,1)S(1)} %get-tuple-element.117), channel_id=1, source_target_pairs={{0,2},{2,4},{4,6},{6,8},{8,10},{10,12},{12,14},{14,16},{16,18},{18... | collective-permute-start | bytes 24584 | tf_op jit(solution)/shard_map/ppermute | solution.py:13
  97.7 7.4 %collective-permute-start.19 = (bf16[32,1,128]{2,0,1:T(8,128)(2,1)S(1)}, bf16[32,1,128]{2,0,1:T(8,128)(2,1)S(1)}, u32[]{:S(2)}, u32[]{:S(2)}) collective-permute-start(bf16[32,1,128]{2,0,1:T(8,128)(2,1)S(1)} %slice.380), channel_id=1, source_target_pairs={{2,0},{4,2},{6,4},{8,6},{10,8},{12,10},{14,12},{16,14},{18,16},{20... | collective-permute-start | bytes 24584 | tf_op jit(solution)/shard_map/ppermute | solution.py:13
  99.7 6.9 %collective-permute-start.23 = (bf16[32,8,128]{2,0,1:T(8,128)(2,1)S(1)}, bf16[32,8,128]{2,0,1:T(8,128)(2,1)S(1)}, u32[]{:S(2)}, u32[]{:S(2)}) collective-permute-start(bf16[32,8,128]{2,0,1:T(8,128)(2,1)S(1)} %maximum_select_fusion.11), channel_id=1, source_target_pairs={{0,16},{2,18},{4,20},{6,22},{8,24},{10,26},{12,28},{14,30},{16,0},... | collective-permute-start | bytes 196616 | tf_op jit(solution)/shard_map/ppermute | solution.py:31
  119.4 6.8 %collective-permute-start.28 = (bf16[32,4,128]{2,0,1:T(8,128)(2,1)S(1)}, bf16[32,4,128]{2,0,1:T(8,128)(2,1)S(1)}, u32[]{:S(2)}, u32[]{:S(2)}) collective-permute-start(bf16[32,4,128]{2,0,1:T(8,128)(2,1)S(1)} %maximum_select_fusion.20), channel_id=1, source_target_pairs={{0,8},{2,10},{4,12},{6,14},{8,0},{10,2},{12,4},{14,6},{16,24},{18,... | collective-permute-start | bytes 98312 | tf_op jit(solution)/shard_map/ppermute | solution.py:31
  120.1 7.5 %collective-permute-start.24 = (bf16[32,1,128]{2,0,1:T(8,128)(2,1)S(1)}, bf16[32,1,128]{2,0,1:T(8,128)(2,1)S(1)}, u32[]{:S(2)}, u32[]{:S(2)}) collective-permute-start(bf16[32,1,128]{2,0,1:T(8,128)(2,1)S(1)} %get-tuple-element.114), channel_id=1, source_target_pairs={{0,2},{2,4},{4,6},{6,8},{8,10},{10,12},{12,14},{14,16},{16,18},{18... | collective-permute-start | bytes 24584 | tf_op jit(solution)/shard_map/ppermute | solution.py:13
  124.1 7.3 %collective-permute-start.25 = (bf16[32,1,128]{2,0,1:T(8,128)(2,1)S(1)}, bf16[32,1,128]{2,0,1:T(8,128)(2,1)S(1)}, u32[]{:S(2)}, u32[]{:S(2)}) collective-permute-start(bf16[32,1,128]{2,0,1:T(8,128)(2,1)S(1)} %slice.386), channel_id=1, source_target_pairs={{2,0},{4,2},{6,4},{8,6},{10,8},{12,10},{14,12},{16,14},{18,16},{20... | collective-permute-start | bytes 24584 | tf_op jit(solution)/shard_map/ppermute | solution.py:13
  126.2 6.7 %collective-permute-start.29 = (bf16[32,8,128]{2,0,1:T(8,128)(2,1)S(1)}, bf16[32,8,128]{2,0,1:T(8,128)(2,1)S(1)}, u32[]{:S(2)}, u32[]{:S(2)}) collective-permute-start(bf16[32,8,128]{2,0,1:T(8,128)(2,1)S(1)} %maximum_select_fusion.12), channel_id=1, source_target_pairs={{0,16},{2,18},{4,20},{6,22},{8,24},{10,26},{12,28},{14,30},{16,0},... | collective-permute-start | bytes 196616 | tf_op jit(solution)/shard_map/ppermute | solution.py:31
  145.0 8.9 %collective-permute-start.34 = (bf16[32,4,128]{2,0,1:T(8,128)(2,1)S(1)}, bf16[32,4,128]{2,0,1:T(8,128)(2,1)S(1)}, u32[]{:S(2)}, u32[]{:S(2)}) collective-permute-start(bf16[32,4,128]{2,0,1:T(8,128)(2,1)S(1)} %maximum_select_fusion.21), channel_id=1, source_target_pairs={{0,8},{2,10},{4,12},{6,14},{8,0},{10,2},{12,4},{14,6},{16,24},{18,... | collective-permute-start | bytes 98312 | tf_op jit(solution)/shard_map/ppermute | solution.py:31
  146.6 8.4 %collective-permute-start.30 = (bf16[32,1,128]{2,0,1:T(8,128)(2,1)S(1)}, bf16[32,1,128]{2,0,1:T(8,128)(2,1)S(1)}, u32[]{:S(2)}, u32[]{:S(2)}) collective-permute-start(bf16[32,1,128]{2,0,1:T(8,128)(2,1)S(1)} %get-tuple-element.111), channel_id=1, source_target_pairs={{0,2},{2,4},{4,6},{6,8},{8,10},{10,12},{12,14},{14,16},{16,18},{18... | collective-permute-start | bytes 24584 | tf_op jit(solution)/shard_map/ppermute | solution.py:13
  152.0 8.1 %collective-permute-start.31 = (bf16[32,1,128]{2,0,1:T(8,128)(2,1)S(1)}, bf16[32,1,128]{2,0,1:T(8,128)(2,1)S(1)}, u32[]{:S(2)}, u32[]{:S(2)}) collective-permute-start(bf16[32,1,128]{2,0,1:T(8,128)(2,1)S(1)} %slice.392), channel_id=1, source_target_pairs={{2,0},{4,2},{6,4},{8,6},{10,8},{12,10},{14,12},{16,14},{18,16},{20... | collective-permute-start | bytes 24584 | tf_op jit(solution)/shard_map/ppermute | solution.py:13
  153.9 7.6 %collective-permute-start.35 = (bf16[32,8,128]{2,0,1:T(8,128)(2,1)S(1)}, bf16[32,8,128]{2,0,1:T(8,128)(2,1)S(1)}, u32[]{:S(2)}, u32[]{:S(2)}) collective-permute-start(bf16[32,8,128]{2,0,1:T(8,128)(2,1)S(1)} %maximum_select_fusion.13), channel_id=1, source_target_pairs={{0,16},{2,18},{4,20},{6,22},{8,24},{10,26},{12,28},{14,30},{16,0},... | collective-permute-start | bytes 196616 | tf_op jit(solution)/shard_map/ppermute | solution.py:31
  174.3 6.5 %collective-permute-start.40 = (bf16[32,4,128]{2,0,1:T(8,128)(2,1)S(1)}, bf16[32,4,128]{2,0,1:T(8,128)(2,1)S(1)}, u32[]{:S(2)}, u32[]{:S(2)}) collective-permute-start(bf16[32,4,128]{2,0,1:T(8,128)(2,1)S(1)} %maximum_select_fusion.22), channel_id=1, source_target_pairs={{0,8},{2,10},{4,12},{6,14},{8,0},{10,2},{12,4},{14,6},{16,24},{18,... | collective-permute-start | bytes 98312 | tf_op jit(solution)/shard_map/ppermute | solution.py:31
  175.0 6.7 %collective-permute-start.36 = (bf16[32,1,128]{2,0,1:T(8,128)(2,1)S(1)}, bf16[32,1,128]{2,0,1:T(8,128)(2,1)S(1)}, u32[]{:S(2)}, u32[]{:S(2)}) collective-permute-start(bf16[32,1,128]{2,0,1:T(8,128)(2,1)S(1)} %get-tuple-element.108), channel_id=1, source_target_pairs={{0,2},{2,4},{4,6},{6,8},{8,10},{10,12},{12,14},{14,16},{16,18},{18... | collective-permute-start | bytes 24584 | tf_op jit(solution)/shard_map/ppermute | solution.py:13
  178.5 7.3 %collective-permute-start.37 = (bf16[32,1,128]{2,0,1:T(8,128)(2,1)S(1)}, bf16[32,1,128]{2,0,1:T(8,128)(2,1)S(1)}, u32[]{:S(2)}, u32[]{:S(2)}) collective-permute-start(bf16[32,1,128]{2,0,1:T(8,128)(2,1)S(1)} %slice.398), channel_id=1, source_target_pairs={{2,0},{4,2},{6,4},{8,6},{10,8},{12,10},{14,12},{16,14},{18,16},{20... | collective-permute-start | bytes 24584 | tf_op jit(solution)/shard_map/ppermute | solution.py:13
  180.8 6.5 %collective-permute-start.41 = (bf16[32,8,128]{2,0,1:T(8,128)(2,1)S(1)}, bf16[32,8,128]{2,0,1:T(8,128)(2,1)S(1)}, u32[]{:S(2)}, u32[]{:S(2)}) collective-permute-start(bf16[32,8,128]{2,0,1:T(8,128)(2,1)S(1)} %maximum_select_fusion.14), channel_id=1, source_target_pairs={{0,16},{2,18},{4,20},{6,22},{8,24},{10,26},{12,28},{14,30},{16,0},... | collective-permute-start | bytes 196616 | tf_op jit(solution)/shard_map/ppermute | solution.py:31
  199.4 8.7 %collective-permute-start.46 = (bf16[32,4,128]{2,0,1:T(8,128)(2,1)S(1)}, bf16[32,4,128]{2,0,1:T(8,128)(2,1)S(1)}, u32[]{:S(2)}, u32[]{:S(2)}) collective-permute-start(bf16[32,4,128]{2,0,1:T(8,128)(2,1)S(1)} %maximum_select_fusion.23), channel_id=1, source_target_pairs={{0,8},{2,10},{4,12},{6,14},{8,0},{10,2},{12,4},{14,6},{16,24},{18,... | collective-permute-start | bytes 98312 | tf_op jit(solution)/shard_map/ppermute | solution.py:31
  201.2 7.9 %collective-permute-start.42 = (bf16[32,1,128]{2,0,1:T(8,128)(2,1)S(1)}, bf16[32,1,128]{2,0,1:T(8,128)(2,1)S(1)}, u32[]{:S(2)}, u32[]{:S(2)}) collective-permute-start(bf16[32,1,128]{2,0,1:T(8,128)(2,1)S(1)} %get-tuple-element.105), channel_id=1, source_target_pairs={{0,2},{2,4},{4,6},{6,8},{8,10},{10,12},{12,14},{14,16},{16,18},{18... | collective-permute-start | bytes 24584 | tf_op jit(solution)/shard_map/ppermute | solution.py:13
  206.2 7.3 %collective-permute-start.43 = (bf16[32,1,128]{2,0,1:T(8,128)(2,1)S(1)}, bf16[32,1,128]{2,0,1:T(8,128)(2,1)S(1)}, u32[]{:S(2)}, u32[]{:S(2)}) collective-permute-start(bf16[32,1,128]{2,0,1:T(8,128)(2,1)S(1)} %slice.404), channel_id=1, source_target_pairs={{2,0},{4,2},{6,4},{8,6},{10,8},{12,10},{14,12},{16,14},{18,16},{20... | collective-permute-start | bytes 24584 | tf_op jit(solution)/shard_map/ppermute | solution.py:13
  208.2 6.8 %collective-permute-start.47 = (bf16[32,8,128]{2,0,1:T(8,128)(2,1)S(1)}, bf16[32,8,128]{2,0,1:T(8,128)(2,1)S(1)}, u32[]{:S(2)}, u32[]{:S(2)}) collective-permute-start(bf16[32,8,128]{2,0,1:T(8,128)(2,1)S(1)} %maximum_select_fusion.15), channel_id=1, source_target_pairs={{0,16},{2,18},{4,20},{6,22},{8,24},{10,26},{12,28},{14,30},{16,0},... | collective-permute-start | bytes 196616 | tf_op jit(solution)/shard_map/ppermute | solution.py:31
  (29 other events, 119.5 us)
